TPU v7x, 128 devices: a whole 4x4x4 slice. The times are simulated.
128 devices in a mesh: xs: 16 (over y, z), ys: 8 (over x, core).
Axes of the slice: x: 4, y: 4, z: 4, core: 2. Of those that a mesh axis runs over, the one named last changes fastest.
Arguments:
- multipoles: bfloat16 [121, 16384], P(None, ('xs', 'ys')), may hold values from -6 to 6
- translation_ops: bfloat16 [316, 121, 121], replicated, may hold values from -0.046875 to 0.046875
- target_interaction_table: int32 [316, 16384], P(None, ('xs', 'ys')), may hold values from -1 to 1151, as said below
- evaluation: bfloat16 [4, 121, 262144], P(None, None, ('xs', 'ys')), may hold values from -0.5 to 0.5
- ion_data: bfloat16 [4, 262144], P(None, ('xs', 'ys')), may hold values from -1 to 1
- atom_owner: int32 [262144, 1], P(('xs', 'ys')), may hold values from 0 to 127, as said below
- atom_slot: int32 [262144], P(('xs', 'ys')), may hold values from 0 to 127
Outputs:
- local_exp: bfloat16 [121, 16384], P(None, ('xs', 'ys'))
- atom_far_field: float32 [4, 262144], P(None, ('xs', 'ys'))
- box_virial: float32 [9, 16384], P(None, ('xs', 'ys'))
Inputs may be any that keep to these rules, and one draw needn't show every extreme that they name: `target_interaction_table`: box slot s of a device is (bx * 4 + by) * 8 + bz; device (ix, iy) holds the periodic grid's boxes of x from ix * 4, y from iy * 4 and all z. Row k stands for the k-th offset (dx, dy, dz) of -3..3 in each coordinate, dx slowest, dz fastest, leaving out those with all three of magnitude 1 or less. An entry is -1, or (3 * (ex + 1) + (ey + 1)) * 128 + s naming the box at that offset from the target: slot s of the device ex steps along xs and ey steps along ys away, ex and ey in -1, 0, 1. It is -1 where the offset along some coordinate lies outside -2 - q .. 3 - q, q the parity of the target's coordinate there, and where the box at that offset holds no ions; most boxes hold ions. `atom_owner`: the device is ix * 8 + iy; an atom held by device (ix, iy) names that device itself or one of the eight devices ((ix + ex) mod 16, (iy + ey) mod 8) with ex, ey in -1, 0, 1; among the atoms of one device at most 32 name the same other device, and in every device's atoms some other device is named exactly 32 times.
All inputs are finite; a program needn't handle non-finite values.
Results may differ from a plain program's by a relative error of at most 0.0029.
Values may be sent and summed in bfloat16 or wider, within the bound.
A program may use at most 64 MiB of HBM per device.

v0:
```python
import jax
import jax.numpy as jnp
from jax import lax
from jax.sharding import PartitionSpec as P


def extended_2(block, sides, width):
    for axis, dim in sides:
        count = lax.axis_size(axis)
        forward = [(i, i + 1) for i in range(count - 1)]
        forward.append((count - 1, 0))
        backward = [(target, source) for source, target in forward]
        low = lax.ppermute(
            lax.slice_in_dim(block, block.shape[dim] - width, None, axis=dim), axis, forward
        )
        high = lax.ppermute(lax.slice_in_dim(block, 0, width, axis=dim), axis, backward)
        block = jnp.concatenate([low, block, high], axis=dim)
    return block


def virial_of(ions, values):
    charge = ions[0].astype(jnp.float32)
    position = ions[1:4].astype(jnp.float32)
    combined = charge[None, None, :] * position[:, None, :] * values[None, 1:4, :]
    return combined.reshape(9, values.shape[1])


def box_sums(virial_terms, safe_slots, capacity):
    summed = jax.ops.segment_sum(virial_terms.T, safe_slots, num_segments=capacity + 1)
    return summed[:capacity].T


def scatter_cols(source_box_index, place, incoming_row_data, fill_value, dtype):
    start = jnp.full((source_box_index.shape[0], incoming_row_data + 1), fill_value, dtype)
    return start.at[:, place].set(source_box_index)[:, :incoming_row_data]


def as_grid(buffer):
    return buffer.reshape(buffer.shape[0], 3, 3, buffer.shape[1] // 9)


def from_grid(extended):
    picked = extended[:, 0::2, 0::2, :]
    return picked.reshape(picked.shape[0], 9 * picked.shape[3])


def shards(
    multipoles,
    translation_ops,
    target_interaction_table,
    evaluation,
    ion_data,
    atom_owner,
    atom_slot,
):
    num_terms, capacity = multipoles.shape
    size_x = lax.axis_size("xs")
    size_y = lax.axis_size("ys")
    atoms_dev = atom_slot.shape[0]
    per_peer = atoms_dev // 64
    incoming_row_data = 9 * per_peer
    extended = extended_2(multipoles.reshape(num_terms, 1, 1, capacity), (("xs", 1), ("ys", 2)), 1)
    columns = jnp.concatenate(
        [extended.reshape(num_terms, 9 * capacity), jnp.zeros((num_terms, 1), jnp.bfloat16)], axis=1
    )
    entries = target_interaction_table
    entries = jnp.where(entries < 0, 9 * capacity, entries)
    gathered = jnp.take(columns, entries, axis=1)
    pieces = jnp.einsum(
        "kqp,pkt->qt", translation_ops, gathered, preferred_element_type=jnp.float32
    )
    local_exp = pieces.astype(jnp.bfloat16)
    padded_local = jnp.concatenate([local_exp, jnp.zeros((num_terms, 1), jnp.bfloat16)], axis=1)
    owners = atom_owner[:, 0]
    myself = lax.axis_index(("xs", "ys"))
    mine_x = myself // size_y
    mine_y = myself % size_y
    step_x = (owners // size_y - mine_x + 1) % size_x - 1
    stride_along_y = (owners % size_y - mine_y + 1) % size_y - 1
    offset = 3 * (step_x + 1) + stride_along_y + 1
    remote = owners != myself
    member = (
        (offset[:, None] == jnp.arange(9, dtype=jnp.int32)[None, :]) & remote[:, None]
    ).astype(jnp.int32)
    previous_level = jnp.cumsum(member, axis=0) - member
    place = jnp.where(
        remote, offset * per_peer + jnp.sum(previous_level * member, axis=1), incoming_row_data
    )
    local_slots = jnp.where(remote, capacity, atom_slot)
    own_cols = jnp.take(padded_local, atom_slot, axis=1)
    requests = scatter_cols(atom_slot[None, :], place, incoming_row_data, -1, jnp.int32)
    slots = from_grid(extended_2(as_grid(requests), (("xs", 1), ("ys", 2)), 1))[0]
    safe_slots = jnp.where(slots < 0, capacity, slots)
    box_cols = jnp.take(padded_local, safe_slots, axis=1)
    returned = from_grid(extended_2(as_grid(box_cols), (("xs", 1), ("ys", 2)), 1))
    returned = jnp.concatenate([returned, jnp.zeros((num_terms, 1), jnp.bfloat16)], axis=1)
    far_cols = jnp.take(returned, place, axis=1)
    atom_column_list = jnp.where(remote[None, :], far_cols, own_cols)
    atom_far_field = jnp.einsum(
        "zuq,uq->zq", evaluation, atom_column_list, preferred_element_type=jnp.float32
    )
    terms = virial_of(ion_data, atom_far_field)
    outgoing = scatter_cols(terms, place, incoming_row_data, 0.0, jnp.float32)
    incoming = from_grid(extended_2(as_grid(outgoing), (("xs", 1), ("ys", 2)), 1))
    box_virial = box_sums(incoming, safe_slots, capacity) + box_sums(terms, local_slots, capacity)
    return (local_exp, atom_far_field, box_virial)


def solution(mesh):
    placed = (
        P(None, ("xs", "ys")),
        P(),
        P(None, ("xs", "ys")),
        P(None, None, ("xs", "ys")),
        P(None, ("xs", "ys")),
        P(("xs", "ys"), None),
        P(("xs", "ys")),
    )
    return jax.shard_map(
        shards,
        mesh=mesh,
        in_specs=placed,
        out_specs=(P(None, ("xs", "ys")), P(None, ("xs", "ys")), P(None, ("xs", "ys"))),
        check_vma=False,
    )
```

profile of v0, /device:TPU:0, one launch (start us, length us, event | category | flops | bytes accessed | tf_op | source)
XLA Modules:
  0.0 200.5 jit_solution(14426252791401849390)
XLA Ops:
  0.6 6.6 %collective-permute-start.1 = (bf16[121,1,1,128]{3,0,2,1:T(8,128)(2,1)}, bf16[121,1,1,128]{3,0,2,1:T(8,128)(2,1)S(1)}, u32[]{:S(2)}, u32[]{:S(2)}) collective-permute-start(bf16[121,1,1,128]{3,0,2,1:T(8,128)(2,1)} %bitcast.73), channel_id=1, source_target_pairs={{8,0},{16,8},{24,16},{32,24},{40,32},{48,40},{56,48},{64,56},{72,6... | collective-permute-start | bytes 92936 | tf_op jit(solution)/shard_map/ppermute | solution.py:16
  8.9 2.6 %reduce-window.6 = s32[9,16,128]{2,1,0:T(8,128)S(1)} reduce-window(s32[9,16,128]{2,1,0:T(8,128)S(1)} %fusion.31, s32[]{:T(128)} %constant.127.clone.1), window={size=1x1x128 pad=0_0x0_0x127_0}, to_apply=%region_0.1 | reduce-window | flops 2340864 | bytes 147460 | tf_op jit(solution)/shard_map/reduce-window
  13.0 8.2 %scatter_custom_fusion = s32[289]{0:T(512)S(1)} fusion(s32[2048]{0:T(1024)S(1)} %bitcast.83, s32[2048]{0:T(1024)} %param.13, s32[]{:T(128)} %constant.139.clone.1), kind=kCustom, calls=%fused_computation.98 | custom fusion | bytes 1668 | tf_op jit(solution)/shard_map/scatter | solution.py:35
  21.4 5.4 %collective-permute-start.5 = (s32[1,1,3,32]{3,2,1,0:T(4,128)S(1)}, s32[1,1,3,32]{3,2,1,0:T(4,128)S(1)}, u32[]{:S(2)}, u32[]{:S(2)}) collective-permute-start(s32[1,1,3,32]{3,2,1,0:T(4,128)S(1)} %get-tuple-element.28), channel_id=1, source_target_pairs={{8,0},{16,8},{24,16},{32,24},{40,32},{48,40},{56,48},{64,56},{72,6... | collective-permute-start | bytes 1160 | tf_op jit(solution)/shard_map/ppermute | solution.py:16
  29.3 1.4 collective-permute-start.7
  32.0 2.9 %collective-permute-done.6 = s32[1,5,1,32]{3,2,1,0:T(1,128)S(1)} collective-permute-done((s32[1,5,1,32]{3,2,1,0:T(1,128)S(1)}, s32[1,5,1,32]{3,2,1,0:T(1,128)S(1)}, u32[]{:S(2)}, u32[]{:S(2)}) %collective-permute-start.6) | collective-permute-done | bytes 672 | tf_op jit(solution)/shard_map/ppermute | solution.py:13
  36.5 1.7 collective-permute-done.3
  38.2 3.1 %collective-permute-done.2 = bf16[121,3,1,128]{3,0,2,1:T(8,128)(2,1)S(1)} collective-permute-done((bf16[121,3,1,128]{3,0,2,1:T(8,128)(2,1)S(1)}, bf16[121,3,1,128]{3,0,2,1:T(8,128)(2,1)S(1)}, u32[]{:S(2)}, u32[]{:S(2)}) %collective-permute-start.2) | collective-permute-done | bytes 92960 | tf_op jit(solution)/shard_map/ppermute | solution.py:13
  42.4 81.1 %gather_fusion = bf16[40448,121]{1,0:T(8,128)(2,1)} fusion(bf16[121,1153]{0,1:T(8,128)(2,1)S(1)} %concatenate.35, s32[40960]{0:T(1024)S(1)} %pad_clamp_fusion), kind=kCustom, calls=%fused_computation | custom fusion | bytes 19738624 | tf_op jit(solution)/shard_map/jit(_take)/gather | solution.py:68
  123.4 16.7 %fusion.16 = bf16[121,128]{0,1:T(8,128)(2,1)S(1)} fusion(bf16[316,121,121]{2,0,1:T(8,128)(2,1)} %param.8, bf16[316,128,121]{2,1,0:T(8,128)(2,1)} %bitcast.63, pred[316,128]{1,0:T(8,128)(4,1)S(1)} %compare_and_fusion), kind=kOutput, calls=%fused_computation.17 | convolution fusion | flops 1189308032 | bytes 19112952 | tf_op jit(solution)/shard_map/kqp,pkt->qt/dot_general | solution.py:69
  140.2 1.4 gather_fusion.1
  141.7 3.6 %collective-permute-start.9 = (bf16[121,1,3,32]{0,3,2,1:T(8,128)(2,1)S(1)}, bf16[121,1,3,32]{0,3,2,1:T(8,128)(2,1)S(1)}, u32[]{:S(2)}, u32[]{:S(2)}) collective-permute-start(bf16[121,1,3,32]{0,3,2,1:T(8,128)(2,1)S(1)} %get-tuple-element.21), channel_id=1, source_target_pairs={{8,0},{16,8},{24,16},{32,24},{40,32},{48,40},{56,48},{64,56},{72,6... | collective-permute-start | bytes 69704 | tf_op jit(solution)/shard_map/ppermute | solution.py:16
  145.3 1.5 collective-permute-done.9
  146.8 5.6 %collective-permute-done.8 = bf16[121,1,3,32]{0,3,2,1:T(8,128)(2,1)S(1)} collective-permute-done((bf16[121,1,3,32]{0,3,2,1:T(8,128)(2,1)S(1)}, bf16[121,1,3,32]{0,3,2,1:T(8,128)(2,1)S(1)}, u32[]{:S(2)}, u32[]{:S(2)}) %collective-permute-start.8) | collective-permute-done | bytes 23264 | tf_op jit(solution)/shard_map/ppermute | solution.py:13
  153.0 6.2 %gather_fusion.3 = bf16[2048,121]{1,0:T(8,128)(2,1)S(1)} fusion(bf16[121,129]{0,1:T(8,128)(2,1)S(1)} %concatenate.38, s32[2048]{0:T(1024)S(1)} %get-tuple-element.27), kind=kCustom, calls=%fused_computation.3 | custom fusion | bytes 999424 | tf_op jit(solution)/shard_map/jit(_take)/gather | solution.py:90
  159.3 6.2 %gather_fusion.2 = bf16[2048,121]{1,0:T(8,128)(2,1)S(1)} fusion(bf16[121,289]{0,1:T(8,128)(2,1)S(1)} %concatenate.41, s32[2048]{0:T(1024)S(1)} %get-tuple-element.30), kind=kCustom, calls=%fused_computation.2 | custom fusion | bytes 999424 | tf_op jit(solution)/shard_map/jit(_take)/gather | solution.py:97
  166.9 2.7 %multiply_reduce_fusion = f32[2048,4]{0,1:T(4,128)S(1)} fusion(f32[2048,121]{0,1:T(8,128)S(1)} %copy.38, bf16[4,121,2048]{2,0,1:T(4,128)(2,1)} %param.10), kind=kLoop, calls=%fused_computation.14 | loop fusion | flops 2965504 | bytes 3006464 | tf_op jit(solution)/shard_map/zuq,uq->zq/dot_general | solution.py:99
  170.1 5.7 %scatter_custom_fusion.1 = f32[9,289]{0,1:T(8,128)S(1)} fusion(s32[2048]{0:T(1024)S(1)} %bitcast.85, f32[9,2048]{0,1:T(8,128)S(1)} %copy.23, f32[]{:T(128)} %constant.147.clone.1), kind=kCustom, calls=%fused_computation.20 | custom fusion | bytes 1058984 | tf_op jit(solution)/shard_map/scatter | solution.py:35
  176.0 2.0 %collective-permute-start.12 = (f32[9,1,3,32]{3,2,1,0:T(4,128)S(1)}, f32[9,1,3,32]{3,2,1,0:T(4,128)S(1)}, u32[]{:S(2)}, u32[]{:S(2)}) collective-permute-start(f32[9,1,3,32]{3,2,1,0:T(4,128)S(1)} %get-tuple-element.22), channel_id=1, source_target_pairs={{0,8},{8,16},{16,24},{24,32},{32,40},{40,48},{48,56},{56,64},{64,7... | collective-permute-start | bytes 10376 | tf_op jit(solution)/shard_map/ppermute | solution.py:13
  178.0 1.7 collective-permute-done.13
  179.8 3.6 %collective-permute-done.12 = f32[9,1,3,32]{3,2,1,0:T(4,128)S(1)} collective-permute-done((f32[9,1,3,32]{3,2,1,0:T(4,128)S(1)}, f32[9,1,3,32]{3,2,1,0:T(4,128)S(1)}, u32[]{:S(2)}, u32[]{:S(2)}) %collective-permute-start.12) | collective-permute-done | bytes 3488 | tf_op jit(solution)/shard_map/ppermute | solution.py:13
  183.4 1.3 collective-permute-start.15
  185.5 11.5 %scatter_custom_fusion.3 = f32[129,9]{1,0:T(8,128)S(1)} fusion(s32[2048]{0:T(1024)S(1)} %get-tuple-element.26, f32[9,2048]{0,1:T(8,128)S(1)} %copy.23, f32[]{:T(128)} %constant.147.clone.1), kind=kCustom, calls=%fused_computation.18 | custom fusion | flops 18432 | bytes 1053224 | tf_op jit(solution)/shard_map/scatter-add | solution.py:29
  198.2 1.7 scatter_custom_fusion.2
  (81 shorter events, 15.1 us)
Async XLA Ops:
  0.6 34.5 %collective-permute-start.1 = (bf16[121,1,1,128]{3,0,2,1:T(8,128)(2,1)}, bf16[121,1,1,128]{3,0,2,1:T(8,128)(2,1)S(1)}, u32[]{:S(2)}, u32[]{:S(2)}) collective-permute-start(bf16[121,1,1,128]{3,0,2,1:T(8,128)(2,1)} %bitcast.73), channel_id=1, source_target_pairs={{8,0},{16,8},{24,16},{32,24},{40,32},{48,40},{56,48},{64,56},{72,6... | collective-permute-start | bytes 92936 | tf_op jit(solution)/shard_map/ppermute | solution.py:16
  7.3 27.9 %collective-permute-start = (bf16[121,1,1,128]{3,0,2,1:T(8,128)(2,1)}, bf16[121,1,1,128]{3,0,2,1:T(8,128)(2,1)S(1)}, u32[]{:S(2)}, u32[]{:S(2)}) collective-permute-start(bf16[121,1,1,128]{3,0,2,1:T(8,128)(2,1)} %bitcast.74), channel_id=1, source_target_pairs={{0,8},{8,16},{16,24},{24,32},{32,40},{40,48},{48,56},{56,64},{64,7... | collective-permute-start | bytes 92936 | tf_op jit(solution)/shard_map/ppermute | solution.py:13
  21.4 7.9 %collective-permute-start.4 = (s32[1,1,3,32]{3,2,1,0:T(4,128)S(1)}, s32[1,1,3,32]{3,2,1,0:T(4,128)S(1)}, u32[]{:S(2)}, u32[]{:S(2)}) collective-permute-start(s32[1,1,3,32]{3,2,1,0:T(4,128)S(1)} %get-tuple-element.29), channel_id=1, source_target_pairs={{0,8},{8,16},{16,24},{24,32},{32,40},{40,48},{48,56},{56,64},{64,7... | collective-permute-start | bytes 1160 | tf_op jit(solution)/shard_map/ppermute | solution.py:13
  21.4 7.9 %collective-permute-start.5 = (s32[1,1,3,32]{3,2,1,0:T(4,128)S(1)}, s32[1,1,3,32]{3,2,1,0:T(4,128)S(1)}, u32[]{:S(2)}, u32[]{:S(2)}) collective-permute-start(s32[1,1,3,32]{3,2,1,0:T(4,128)S(1)} %get-tuple-element.28), channel_id=1, source_target_pairs={{8,0},{16,8},{24,16},{32,24},{40,32},{48,40},{56,48},{64,56},{72,6... | collective-permute-start | bytes 1160 | tf_op jit(solution)/shard_map/ppermute | solution.py:16
  29.3 2.7 %collective-permute-start.7 = (s32[1,5,1,32]{3,2,1,0:T(1,128)S(1)}, s32[1,5,1,32]{3,2,1,0:T(1,128)S(1)}, u32[]{:S(2)}, u32[]{:S(2)}) collective-permute-start(s32[1,5,1,32]{3,2,1,0:T(1,128)S(1)} %get-tuple-element.25), channel_id=1, source_target_pairs={{1,0},{2,1},{3,2},{4,3},{5,4},{6,5},{7,6},{0,7},{9,8},{10,9},{11,1... | collective-permute-start | bytes 1928 | tf_op jit(solution)/shard_map/ppermute | solution.py:16
  30.7 4.2 %collective-permute-start.6 = (s32[1,5,1,32]{3,2,1,0:T(1,128)S(1)}, s32[1,5,1,32]{3,2,1,0:T(1,128)S(1)}, u32[]{:S(2)}, u32[]{:S(2)}) collective-permute-start(s32[1,5,1,32]{3,2,1,0:T(1,128)S(1)} %get-tuple-element.24), channel_id=1, source_target_pairs={{0,1},{1,2},{2,3},{3,4},{4,5},{5,6},{6,7},{7,0},{8,9},{9,10},{10,1... | collective-permute-start | bytes 1928 | tf_op jit(solution)/shard_map/ppermute | solution.py:13
  36.0 2.2 %collective-permute-start.3 = (bf16[121,3,1,128]{3,0,2,1:T(8,128)(2,1)S(1)}, bf16[121,3,1,128]{3,0,2,1:T(8,128)(2,1)S(1)}, u32[]{:S(2)}, u32[]{:S(2)}) collective-permute-start(bf16[121,3,1,128]{3,0,2,1:T(8,128)(2,1)S(1)} %pad_maximum_fusion.3), channel_id=1, source_target_pairs={{1,0},{2,1},{3,2},{4,3},{5,4},{6,5},{7,6},{0,7},{9,8},{10,9},{11,1... | collective-permute-start | bytes 278792 | tf_op jit(solution)/shard_map/ppermute | solution.py:16
  36.0 5.3 %collective-permute-start.2 = (bf16[121,3,1,128]{3,0,2,1:T(8,128)(2,1)S(1)}, bf16[121,3,1,128]{3,0,2,1:T(8,128)(2,1)S(1)}, u32[]{:S(2)}, u32[]{:S(2)}) collective-permute-start(bf16[121,3,1,128]{3,0,2,1:T(8,128)(2,1)S(1)} %pad_maximum_fusion.3), channel_id=1, source_target_pairs={{0,1},{1,2},{2,3},{3,4},{4,5},{5,6},{6,7},{7,0},{8,9},{9,10},{10,1... | collective-permute-start | bytes 278792 | tf_op jit(solution)/shard_map/ppermute | solution.py:13
  123.4 21.9 %copy-start.1 = (s32[2048]{0:T(1024)S(1)}, s32[2048]{0:T(1024)}, u32[]{:S(2)}) copy-start(s32[2048]{0:T(1024)} %param.13) | copy-start | bytes 24580
  141.7 5.1 %collective-permute-start.9 = (bf16[121,1,3,32]{0,3,2,1:T(8,128)(2,1)S(1)}, bf16[121,1,3,32]{0,3,2,1:T(8,128)(2,1)S(1)}, u32[]{:S(2)}, u32[]{:S(2)}) collective-permute-start(bf16[121,1,3,32]{0,3,2,1:T(8,128)(2,1)S(1)} %get-tuple-element.21), channel_id=1, source_target_pairs={{8,0},{16,8},{24,16},{32,24},{40,32},{48,40},{56,48},{64,56},{72,6... | collective-permute-start | bytes 69704 | tf_op jit(solution)/shard_map/ppermute | solution.py:16
  145.3 7.1 %collective-permute-start.8 = (bf16[121,1,3,32]{0,3,2,1:T(8,128)(2,1)S(1)}, bf16[121,1,3,32]{0,3,2,1:T(8,128)(2,1)S(1)}, u32[]{:S(2)}, u32[]{:S(2)}) collective-permute-start(bf16[121,1,3,32]{0,3,2,1:T(8,128)(2,1)S(1)} %get-tuple-element.20), channel_id=1, source_target_pairs={{0,8},{8,16},{16,24},{24,32},{32,40},{40,48},{48,56},{56,64},{64,7... | collective-permute-start | bytes 69704 | tf_op jit(solution)/shard_map/ppermute | solution.py:13
  152.5 6.7 %collective-permute-start.11 = (bf16[121,5,1,32]{0,3,2,1:T(8,128)(2,1)S(1)}, bf16[121,5,1,32]{0,3,2,1:T(8,128)(2,1)S(1)}, u32[]{:S(2)}, u32[]{:S(2)}) collective-permute-start(bf16[121,5,1,32]{0,3,2,1:T(8,128)(2,1)S(1)} %get-tuple-element.17), channel_id=1, source_target_pairs={{1,0},{2,1},{3,2},{4,3},{5,4},{6,5},{7,6},{0,7},{9,8},{10,9},{11,1... | collective-permute-start | bytes 116168 | tf_op jit(solution)/shard_map/ppermute | solution.py:16
  152.5 6.7 %collective-permute-start.10 = (bf16[121,5,1,32]{0,3,2,1:T(8,128)(2,1)S(1)}, bf16[121,5,1,32]{0,3,2,1:T(8,128)(2,1)S(1)}, u32[]{:S(2)}, u32[]{:S(2)}) collective-permute-start(bf16[121,5,1,32]{0,3,2,1:T(8,128)(2,1)S(1)} %get-tuple-element.16), channel_id=1, source_target_pairs={{0,1},{1,2},{2,3},{3,4},{4,5},{5,6},{6,7},{7,0},{8,9},{9,10},{10,1... | collective-permute-start | bytes 116168 | tf_op jit(solution)/shard_map/ppermute | solution.py:13
  169.6 30.9 %copy-start = (f32[2048,4]{0,1:T(4,128)}, f32[2048,4]{0,1:T(4,128)S(1)}, u32[]{:S(2)}) copy-start(f32[2048,4]{0,1:T(4,128)S(1)} %multiply_reduce_fusion) | copy-start | bytes 98308
  175.9 3.8 %collective-permute-start.13 = (f32[9,1,3,32]{3,2,1,0:T(4,128)S(1)}, f32[9,1,3,32]{3,2,1,0:T(4,128)S(1)}, u32[]{:S(2)}, u32[]{:S(2)}) collective-permute-start(f32[9,1,3,32]{3,2,1,0:T(4,128)S(1)} %get-tuple-element.23), channel_id=1, source_target_pairs={{8,0},{16,8},{24,16},{32,24},{40,32},{48,40},{56,48},{64,56},{72,6... | collective-permute-start | bytes 10376 | tf_op jit(solution)/shard_map/ppermute | solution.py:16
  176.0 7.3 %collective-permute-start.12 = (f32[9,1,3,32]{3,2,1,0:T(4,128)S(1)}, f32[9,1,3,32]{3,2,1,0:T(4,128)S(1)}, u32[]{:S(2)}, u32[]{:S(2)}) collective-permute-start(f32[9,1,3,32]{3,2,1,0:T(4,128)S(1)} %get-tuple-element.22), channel_id=1, source_target_pairs={{0,8},{8,16},{16,24},{24,32},{32,40},{40,48},{48,56},{56,64},{64,7... | collective-permute-start | bytes 10376 | tf_op jit(solution)/shard_map/ppermute | solution.py:13
  183.4 13.6 %collective-permute-start.15 = (f32[9,5,1,32]{3,2,1,0:T(1,128)S(1)}, f32[9,5,1,32]{3,2,1,0:T(1,128)S(1)}, u32[]{:S(2)}, u32[]{:S(2)}) collective-permute-start(f32[9,5,1,32]{3,2,1,0:T(1,128)S(1)} %get-tuple-element.19), channel_id=1, source_target_pairs={{1,0},{2,1},{3,2},{4,3},{5,4},{6,5},{7,6},{0,7},{9,8},{10,9},{11,1... | collective-permute-start | bytes 17288 | tf_op jit(solution)/shard_map/ppermute | solution.py:16
  184.7 12.2 %collective-permute-start.14 = (f32[9,5,1,32]{3,2,1,0:T(1,128)S(1)}, f32[9,5,1,32]{3,2,1,0:T(1,128)S(1)}, u32[]{:S(2)}, u32[]{:S(2)}) collective-permute-start(f32[9,5,1,32]{3,2,1,0:T(1,128)S(1)} %get-tuple-element.18), channel_id=1, source_target_pairs={{0,1},{1,2},{2,3},{3,4},{4,5},{5,6},{6,7},{7,0},{8,9},{9,10},{10,1... | collective-permute-start | bytes 17288 | tf_op jit(solution)/shard_map/ppermute | solution.py:13
where the time goes:
time: 202 us; the launch traced here: 201 us
  local copies, waits for them, and re-layouts  113 us (56%)
  other arithmetic  27.6 us (14%)
  starting transfers between devices  21.5 us (11%)
  waiting for transfers between devices  20.5 us (10%)
  matrix products  16.7 us (8%)
    gather x1, local copies, waits for them, and re-layouts, shards(): gathered = jnp.take(columns, entries, axis=1)  81.1 us
    ppermute x8, starting transfers between devices, extended_2(): lax.ppermute(lax.slice_in_dim(block, 0, width, axis=dim), axis, backward)  18.5 us
    dot_general x1, matrix products, shards(): jnp.einsum('kqp,pkt->qt', translation_ops, gathered, preferred_element_ty...  16.7 us
    ppermute x8, waiting for transfers between devices, extended_2(): lax.ppermute(lax.slice_in_dim(block, block.shape[dim] - width, None, axis...  15.2 us
    scatter x3, local copies, waits for them, and re-layouts, scatter_cols(): return start.at[:, place].set(source_box_index)[:, :incoming_row_data]  13.9 us
    scatter-add x2, other arithmetic, box_sums(): jax.ops.segment_sum(virial_terms.T, safe_slots, num_segments=capacity + 1)  13.2 us
    gather x1, local copies, waits for them, and re-layouts, shards(): far_cols = jnp.take(returned, place, axis=1)  6.18 us
    gather x1, local copies, waits for them, and re-layouts, shards(): own_cols = jnp.take(padded_local, atom_slot, axis=1)  6.17 us
  transfers between devices with their start and end apart: 16, of which 8 were waited for; matrix products, arithmetic and copies ran while one was open for 18% of the time, Pallas kernels for 0%

commit v1 on v0

v1 whole, which is shorter than its diff:
```python
import functools

import jax
import jax.numpy as jnp
from jax import lax
from jax.experimental import pallas as pl
from jax.experimental.pallas import tpu as pltpu
from jax.sharding import PartitionSpec as P

MESH = pl.DeviceIdType.MESH
NT = (((1,), (1,)), ((), ()))
NN = (((1,), (0,)), ((), ()))
F32 = jnp.float32
BF16 = jnp.bfloat16

AROUND = [(ex, ey) for ex in (-1, 0, 1) for ey in (-1, 0, 1) if (ex, ey) != (0, 0)]


def offset_columns():
    listed, row = [], 0
    for dx in range(-3, 4):
        for dy in range(-3, 4):
            near = abs(dx) <= 1 and abs(dy) <= 1
            listed.append((dx, dy, row, near))
            row += 4 if near else 7
    return listed


COLUMNS = offset_columns()
SELF_ROW = [c[2] for c in COLUMNS if c[:2] == (0, 0)][0] + 1
CHUNKS = [(0, 32), (32, 32), (64, 32), (96, 25)]


def iota(shape, axis):
    return lax.broadcasted_iota(jnp.int32, shape, axis)


def one_hot(condition):
    return jnp.where(condition, 1.0, 0.0).astype(BF16)


def mirror_z(x):
    axis = x.ndim - 1
    lane = iota(x.shape, axis)
    for bit in (1, 2, 4):
        x = jnp.where((lane & bit) != 0, pltpu.roll(x, bit, axis), pltpu.roll(x, 128 - bit, axis))
    return x


def kernel(
    nx, ny,
    mult, ops, table, ev, ions, owner, slot,
    local_out, field_out, virial_out,
    mraw, trow, iraw, oraw, sraw, eb, tb, F, Ef, R, OH, ext, G,
    msend, mrecv, ec, gmsg, fg, ret, Lrep, fo,
    in_sem, op_sem, s1, r1, s2, r2, s3, r3,
):
    mx = lax.axis_index("xs")
    my = lax.axis_index("ys")

    def peer(g):
        ex, ey = AROUND[g]
        return (lax.rem(mx + ex + nx, nx), lax.rem(my + ey + ny, ny))

    first = SELF_ROW // 8 * 8
    loads = [
        pltpu.make_async_copy(mult, mraw, in_sem.at[0]),
        pltpu.make_async_copy(table.at[pl.ds(first, 8)], trow, in_sem.at[1]),
        pltpu.make_async_copy(owner, oraw, in_sem.at[2]),
        pltpu.make_async_copy(slot, sraw, in_sem.at[3]),
        pltpu.make_async_copy(ions, iraw, in_sem.at[4]),
        pltpu.make_async_copy(ev, eb, in_sem.at[5]),
    ]
    for copy in loads:
        copy.start()
    op_loads = [
        pltpu.make_async_copy(ops.at[pl.ds(q0, n)], tb.at[pl.ds(q0, n)], op_sem.at[c])
        for c, (q0, n) in enumerate(CHUNKS)
    ]
    for copy in op_loads:
        copy.start()

    barrier = pltpu.get_barrier_semaphore()
    for g in range(8):
        pl.semaphore_signal(barrier, inc=1, device_id=peer(g), device_id_type=MESH)

    loads[0].wait()
    loads[1].wait()
    named = trow[SELF_ROW - first:SELF_ROW - first + 1, :]
    lane = iota((1, 128), 1)
    named = jnp.where((lane & 7) < 6, pltpu.roll(named, 126, 1), pltpu.roll(named, 6, 1))
    filled = named >= 0
    pick = one_hot((iota((128, 128), 0) == (iota((128, 128), 1) ^ 7)) & jnp.broadcast_to(filled, (128, 128)))
    turned = lax.dot_general(pick, mraw[...], NT, preferred_element_type=F32)
    msend[...] = jnp.zeros_like(msend)
    msend[:, 0:121] = turned.astype(BF16)

    pl.semaphore_wait(barrier, 8)
    halo = []
    for g in range(8):
        ex = AROUND[g][0]
        rows = pl.ds(32 if ex < 0 else 0, 128 if ex == 0 else 96)
        halo.append(pltpu.make_async_remote_copy(
            src_ref=msend.at[rows], dst_ref=mrecv.at[g, rows], send_sem=s1.at[g], recv_sem=r1.at[g],
            device_id=peer(7 - g), device_id_type=MESH))
        halo[-1].start()

    loads[2].wait()
    loads[3].wait()
    own_id = oraw[...]
    shift = ny.bit_length() - 1
    step_x = (((own_id >> shift) - mx + 1 + nx) & (nx - 1)) - 1
    step_y = (((own_id & (ny - 1)) - my + 1 + ny) & (ny - 1)) - 1
    towards = 3 * (step_x + 1) + step_y + 1
    here = towards == 4
    group = jnp.where(here, -1, 7 - jnp.where(towards > 4, towards - 1, towards))
    member = jnp.where(iota((8, 2048), 0) == group, 1.0, 0.0)
    stacked = jnp.concatenate([member[:, 128 * b:128 * b + 128] for b in range(16)], axis=0)
    stacked_b = stacked.astype(BF16)
    row, col = iota((128, 128), 0), iota((128, 128), 1)
    before = one_hot(row < col)
    earlier = one_hot(((row & 7) == (col & 7)) & ((col >> 3) < (row >> 3)))
    ones = jnp.ones((128, 128), BF16)
    counts = lax.dot_general(earlier, stacked_b, NN, preferred_element_type=F32).astype(BF16)
    rank = lax.dot_general(stacked_b, before, NN, preferred_element_type=F32)
    rank = rank + lax.dot_general(counts, ones, NN, preferred_element_type=F32)
    place = stacked * (rank + (32 * (row & 7) + 1).astype(F32))
    place = jnp.sum(place.reshape(16, 8, 128), axis=1, keepdims=True) - 1.0
    row_f = iota((256, 128), 0).astype(F32)
    for b in range(16):
        R[:, 128 * b:128 * b + 128] = one_hot(row_f == place[b])
    own_slot = sraw[...]
    OH[:, 0:2048] = one_hot(iota((128, 2048), 0) == jnp.where(here, own_slot ^ 7, -1))

    loads[4].wait()
    loads[5].wait()

    def spread(i, _):
        both = jnp.concatenate([eb[2 * i].astype(F32), eb[2 * i + 1].astype(F32)], axis=0)
        Ef[pl.ds(pl.multiple_of(8 * i, 8), 8), 0:2048] = both
        return 0

    lax.fori_loop(0, 60, spread, 0, unroll=4)
    Ef[480:488, 0:2048] = jnp.concatenate([eb[120].astype(F32), iraw[...].astype(F32)], axis=0)
    Ef[488:496, 0:2048] = jnp.where(iota((8, 2048), 0) == 0, own_slot.astype(F32), 0.0)
    Ef[496:512, 0:2048] = jnp.zeros((16, 2048), F32)

    ec[...] = lax.dot_general(
        R[...], Ef[:, 0:2048].astype(BF16), NT, preferred_element_type=F32).astype(BF16)
    guests = []
    for g in range(8):
        rows = pl.ds(32 * g, 32)
        guests.append(pltpu.make_async_remote_copy(
            src_ref=ec.at[rows], dst_ref=gmsg.at[rows], send_sem=s2.at[g], recv_sem=r2.at[g],
            device_id=peer(7 - g), device_id_type=MESH))
        guests[-1].start()

    def widen(c):
        q0, n = CHUNKS[c]
        op_loads[c].wait()
        F[q0:q0 + n, 0:316, 0:121] = tb[q0:q0 + n].astype(F32)

    widen(0)

    def place_block(block, ex, ey):
        block = block.astype(F32).reshape(4, 4, 8, 128)
        sx = {-1: (1, 4, 0), 0: (0, 4, 3), 1: (0, 3, 7)}[ex]
        sy = {-1: (1, 4, 0), 0: (0, 4, 3), 1: (0, 3, 7)}[ey]
        ext[sx[2]:sx[2] + sx[1] - sx[0], sy[2]:sy[2] + sy[1] - sy[0]] = block[sx[0]:sx[1], sy[0]:sy[1]]

    place_block(msend[...], 0, 0)
    for g in range(8):
        halo[g].wait_recv()
        place_block(mrecv[g], *AROUND[g])
    grid_x, grid_y = iota((4, 4, 8, 128), 0), iota((4, 4, 8, 128), 1)
    for j, (dx, dy, _, _) in enumerate(COLUMNS):
        block = ext[dx + 3:dx + 7, dy + 3:dy + 7]
        if abs(dx) == 3:
            block = jnp.where((grid_x & 1) == (0 if dx > 0 else 1), block, 0.0)
        if abs(dy) == 3:
            block = jnp.where((grid_y & 1) == (0 if dy > 0 else 1), block, 0.0)
        G[:, 128 * j:128 * j + 128] = block.reshape(128, 128).astype(BF16)

    cell = (32, 8, 128)
    dz = iota(cell, 1) - 3
    source_z = (iota(cell, 2) & 7) - dz
    inside = (source_z >= 0) & (source_z <= 7)
    odd_z = (iota(cell, 2) & 1) == 0
    valid = (jnp.abs(dz) < 3) | ((dz == -3) & odd_z) | ((dz == 3) & jnp.logical_not(odd_z))
    slots = iota((32, 8, 128), 1)
    in_terms = iota((32, 8, 128), 2) < 121

    def weights(q0, j):
        _, _, k0, near = COLUMNS[j]
        rows = F[q0:q0 + 32, k0:k0 + 8, :]
        if near:
            upper = F[q0:q0 + 32, k0 - 3:k0 + 5, :]
            rows = jnp.where(slots < 2, rows, jnp.where((slots >= 5) & (slots < 7), upper, 0.0))
        return jnp.where(in_terms, rows, 0.0).reshape(256, 128).astype(BF16)

    def translate(c):
        q0, n = CHUNKS[c]
        total = jnp.zeros((256, 128), F32)
        for j in range(0, 49, 2):
            if j + 1 < 49:
                w = jnp.concatenate([weights(q0, j), weights(q0, j + 1)], axis=1)
                total = total + lax.dot_general(w, G[:, 128 * j:128 * j + 256], NT, preferred_element_type=F32)
            else:
                total = total + lax.dot_general(
                    weights(q0, j), G[:, 128 * j:128 * j + 128], NT, preferred_element_type=F32)
        total = total.reshape(cell)
        skewed = pltpu.roll(total, 0, 2, stride=1, stride_axis=1)
        turned = pltpu.roll(skewed, 125, 2)
        wrapped = jnp.where(dz > 0, pltpu.roll(skewed, 117, 2), pltpu.roll(skewed, 5, 2))
        picked = jnp.where(valid, jnp.where(inside, turned, wrapped), 0.0)
        sums = jnp.sum(picked, axis=1, keepdims=True)
        wide = jnp.broadcast_to(sums, cell).reshape(16, 2, 8, 128)
        wide = jnp.where(iota((16, 8, 128), 1) < 4, wide[:, 0], wide[:, 1]).reshape(128, 128)
        if n < 32:
            wide = jnp.where(iota((128, 128), 0) < 4 * n, wide, 0.0)
        Lrep[4 * q0:4 * q0 + 128, :] = wide.astype(BF16)
        return jnp.sum(picked, axis=1)

    def put_local(c, sums):
        q0, n = CHUNKS[c]
        local_out[q0:q0 + n, :] = mirror_z(sums)[0:n].astype(BF16)

    F[121:128] = jnp.zeros((7, 320, 128), F32)
    for c in range(3):
        if c:
            widen(c)
        put_local(c, translate(c))
    widen(3)

    for g in range(8):
        guests[g].wait_recv()
    received = gmsg[...].astype(F32)
    for c in range(4):
        Ef[128 * c:128 * c + 128, 2048:2304] = jnp.transpose(received[:, 128 * c:128 * c + 128])
    guest_slot = Ef[488:489, 2048:2304].astype(jnp.int32) ^ 7
    OH[:, 2048:2304] = one_hot(iota((128, 256), 0) == guest_slot)

    last = translate(3)

    def evaluate(start):
        values = lax.dot_general(
            Lrep[0:496, :], OH[:, start:start + 256], NN, preferred_element_type=F32)
        values = values * Ef[0:496, start:start + 256]
        total = jnp.sum(values.reshape(62, 8, 256), axis=0)
        return total + pltpu.roll(total, 4, 0)

    far = evaluate(2048)
    fo[:, 2048:2304] = far
    fg[0] = far[:, 0:128]
    fg[1] = far[:, 128:256]
    answers = []
    for g in range(8):
        answers.append(pltpu.make_async_remote_copy(
            src_ref=fg.at[g // 4], dst_ref=ret.at[g], send_sem=s3.at[g], recv_sem=r3.at[g],
            device_id=peer(g), device_id_type=MESH))
        answers[-1].start()
    put_local(3, last)
    for b in range(8):
        fo[:, 256 * b:256 * b + 256] = evaluate(256 * b)

    field = fo[...]
    charge = Ef[484:485, :]
    low = iota((8, 2304), 0) < 4
    arm = jnp.where(low, charge * Ef[485:486, :], charge * Ef[486:487, :])
    terms = jnp.concatenate([arm * field, charge * Ef[487:488, :] * field], axis=0)
    high = terms.astype(BF16)
    rest = (terms - high.astype(F32)).astype(BF16)
    sums = lax.dot_general(jnp.concatenate([high, rest], axis=0), OH[...], NT, preferred_element_type=F32)
    sums = mirror_z(sums[0:16] + sums[16:32])
    for a in range(3):
        virial_out[3 * a:3 * a + 3, :] = sums[4 * a + 1:4 * a + 4]

    for g in range(8):
        answers[g].wait_recv()
    quarter = iota((8, 128), 1) >> 5
    tiles = []
    for u in range(2):
        tile = ret[4 * u]
        for v in range(1, 4):
            tile = jnp.where(quarter == v, ret[4 * u + v], tile)
        tiles.append(tile)
    back = jnp.concatenate(tiles, axis=1)
    parts = []
    for _ in range(3):
        parts.append(back.astype(BF16).astype(F32))
        back = back - parts[-1]
    spread_out = lax.dot_general(
        jnp.concatenate(parts, axis=0).astype(BF16), R[...], NN, preferred_element_type=F32)
    total = fo[:, 0:2048] + spread_out[0:8] + spread_out[8:16] + spread_out[16:24]
    field_out[...] = total[0:4]

    for g in range(8):
        halo[g].wait_send()
        guests[g].wait_send()
        answers[g].wait_send()


def shards(mult, ops, table, ev, ions, owner, slot):
    nx, ny = lax.axis_size("xs"), lax.axis_size("ys")
    dma = pltpu.SemaphoreType.DMA
    vmem = pltpu.VMEM
    return pl.pallas_call(
        functools.partial(kernel, nx, ny),
        out_shape=(
            jax.ShapeDtypeStruct((121, 128), BF16),
            jax.ShapeDtypeStruct((4, 2048), F32),
            jax.ShapeDtypeStruct((9, 128), F32),
        ),
        in_specs=[pl.BlockSpec(memory_space=pl.ANY)] * 7,
        out_specs=[pl.BlockSpec(memory_space=pltpu.VMEM)] * 3,
        scratch_shapes=[
            vmem((121, 128), BF16), vmem((8, 128), jnp.int32), vmem((4, 2048), BF16),
            vmem((1, 2048), jnp.int32), vmem((1, 2048), jnp.int32),
            vmem((121, 4, 2048), BF16), vmem((121, 316, 121), BF16), vmem((128, 320, 128), F32),
            vmem((512, 2304), F32), vmem((256, 2048), BF16), vmem((128, 2304), BF16),
            vmem((10, 10, 8, 128), F32), vmem((128, 49 * 128), BF16),
            vmem((128, 128), BF16), vmem((8, 128, 128), BF16), vmem((256, 512), BF16), vmem((256, 512), BF16),
            vmem((2, 8, 128), F32), vmem((8, 8, 128), F32), vmem((512, 128), BF16), vmem((8, 2304), F32),
            dma((6,)), dma((4,)), dma((8,)), dma((8,)), dma((8,)), dma((8,)), dma((8,)), dma((8,)),
        ],
        compiler_params=pltpu.CompilerParams(
            collective_id=0, has_side_effects=True, vmem_limit_bytes=58 * 2**20),
    )(
        mult,
        jnp.transpose(ops, (1, 0, 2)),
        table,
        jnp.transpose(ev, (1, 0, 2)),
        ions,
        jnp.reshape(owner, (1, owner.shape[0])),
        jnp.reshape(slot, (1, slot.shape[0])),
    )


def solution(mesh):
    both = ("xs", "ys")
    placed = (
        P(None, both),
        P(),
        P(None, both),
        P(None, None, both),
        P(None, both),
        P(both, None),
        P(both),
    )
    return jax.shard_map(
        shards,
        mesh=mesh,
        in_specs=placed,
        out_specs=(P(None, both), P(None, both), P(None, both)),
        check_vma=False,
    )
```

time: 202 us -> 35 us (0.17)
  local copies, waits for them, and re-layouts: 113 us -> 4.04 us
  Pallas kernels: 0 us -> 30 us
  other arithmetic: 27.6 us -> 0 us
  starting transfers between devices: 21.5 us -> 0 us
  waiting for transfers between devices: 20.5 us -> 0 us
  matrix products: 16.7 us -> 0 us
    gather x4 -> x0, local copies, waits for them, and re-layouts: 94.8 us -> none  [the longest x1 81.1 us: shards(): gathered = jnp.take(columns, entries, axis=1)]
    pallas_call x0 -> x1, Pallas kernels: none -> 30 us  [shards(): pl.pallas_call(functools.partial(kernel, nx, ny), out_shape=(jax.ShapeDty...]
    ppermute x16 -> x0, starting transfers between devices: 21.5 us -> none  [the longest x8 18.5 us: extended_2(): lax.ppermute(lax.slice_in_dim(block, 0, width, axis=dim), axis, backward)]
    ppermute x16 -> x0, waiting for transfers between devices: 20.5 us -> none  [the longest x8 15.2 us: extended_2(): lax.ppermute(lax.slice_in_dim(block, block.shape[dim] - width, None, axis...]
    dot_general x1 -> x0, matrix products: 16.7 us -> none  [shards(): jnp.einsum('kqp,pkt->qt', translation_ops, gathered, preferred_element_ty...]
    scatter x3 -> x0, local copies, waits for them, and re-layouts: 13.9 us -> none  [scatter_cols(): return start.at[:, place].set(source_box_index)[:, :incoming_row_data]]
    scatter-add x2 -> x0, other arithmetic: 13.2 us -> none  [box_sums(): jax.ops.segment_sum(virial_terms.T, safe_slots, num_segments=capacity + 1)]
    another operation x3 -> x0, other arithmetic: 2.82 us -> none
  transfers between devices with their start and end apart: 16 -> 0, of which waited for: 8 -> 0; matrix products, arithmetic and copies ran while one was open for 18% -> 0% of each run, Pallas kernels for 0% -> 0%
where the time goes in v1:
time: 35 us; the launch traced here: 34.7 us
  Pallas kernels  30 us (86%)
  local copies, waits for them, and re-layouts  4.04 us (12%)
  between operations  0.64 us (2%)
    pallas_call x1, Pallas kernels, shards(): pl.pallas_call(functools.partial(kernel, nx, ny), out_shape=(jax.ShapeDty...  30 us
    unnamed x3, local copies, waits for them, and re-layouts  4.04 us

profile of v1, /device:TPU:0, one launch (start us, length us, event | category | flops | bytes accessed | tf_op | source)
XLA Modules:
  0.0 34.7 jit_solution(7441587118982107723)
XLA Ops:
  0.6 30.0 %shard_map.94 = (bf16[121,128]{1,0:T(8,128)(2,1)}, f32[4,2048]{1,0:T(4,128)}, f32[9,128]{1,0:T(8,128)}) custom-call(bf16[121,128]{1,0:T(8,128)(2,1)} %mult.1, bf16[121,316,121]{2,1,0:T(8,128)(2,1)} %bitcast.4, s32[316,128]{1,0:T(8,128)} %table.1, bf16[121,4,2048]{2,1,0:T(4,128)(2,1)} %bitcast.5, bf16[4,2048]{1,0:T(4,128)(2,1)} %ions.1, s32[1,2048]{1,0:T(1,128)} %bitcast.6, ...), custom_call_target="tpu_custom_call" | custom-call | tf_op jit(solution)/shard_map/pallas_call | solution.py:307
  30.6 1.4 %copy.13 = bf16[121,128]{1,0:T(8,128)(2,1)} copy(bf16[121,128]{1,0:T(8,128)(2,1)} %get-tuple-element.6) | data formatting | bytes 61952
  32.0 1.4 %copy.14 = f32[4,2048]{1,0:T(4,128)} copy(f32[4,2048]{1,0:T(4,128)} %get-tuple-element.7) | data formatting | bytes 65536
  33.4 1.3 %copy.15 = f32[9,128]{1,0:T(8,128)} copy(f32[9,128]{1,0:T(8,128)} %get-tuple-element.8) | data formatting | bytes 9216

commit v2 on v1

--- a/solution.py
+++ b/solution.py
@@ -29,6 +29,7 @@
 COLUMNS = offset_columns()
 SELF_ROW = [c[2] for c in COLUMNS if c[:2] == (0, 0)][0] + 1
 CHUNKS = [(0, 32), (32, 32), (64, 32), (96, 25)]
+STEPS = 25
 
 
 def iota(shape, axis):
@@ -155,12 +156,14 @@
             device_id=peer(7 - g), device_id_type=MESH))
         guests[-1].start()
 
-    def widen(c):
+    def widen(c, step):
         q0, n = CHUNKS[c]
-        op_loads[c].wait()
-        F[q0:q0 + n, 0:316, 0:121] = tb[q0:q0 + n].astype(F32)
-
-    widen(0)
+        low, high = q0 + n * step // STEPS, q0 + n * (step + 1) // STEPS
+        F[low:high, 0:316, 0:121] = tb[low:high].astype(F32)
+
+    op_loads[0].wait()
+    for step in range(STEPS):
+        widen(0, step)
 
     def place_block(block, ex, ey):
         block = block.astype(F32).reshape(4, 4, 8, 128)
@@ -181,56 +184,68 @@
             block = jnp.where((grid_y & 1) == (0 if dy > 0 else 1), block, 0.0)
         G[:, 128 * j:128 * j + 128] = block.reshape(128, 128).astype(BF16)
 
-    cell = (32, 8, 128)
-    dz = iota(cell, 1) - 3
-    source_z = (iota(cell, 2) & 7) - dz
-    inside = (source_z >= 0) & (source_z <= 7)
-    odd_z = (iota(cell, 2) & 1) == 0
-    valid = (jnp.abs(dz) < 3) | ((dz == -3) & odd_z) | ((dz == 3) & jnp.logical_not(odd_z))
-    slots = iota((32, 8, 128), 1)
-    in_terms = iota((32, 8, 128), 2) < 121
-
-    def weights(q0, j):
+    def weights(q0, n, j):
         _, _, k0, near = COLUMNS[j]
-        rows = F[q0:q0 + 32, k0:k0 + 8, :]
+        shape = (n, 8, 128)
+        rows = F[q0:q0 + n, k0:k0 + 8, :]
         if near:
-            upper = F[q0:q0 + 32, k0 - 3:k0 + 5, :]
+            slots = iota(shape, 1)
+            upper = F[q0:q0 + n, k0 - 3:k0 + 5, :]
             rows = jnp.where(slots < 2, rows, jnp.where((slots >= 5) & (slots < 7), upper, 0.0))
-        return jnp.where(in_terms, rows, 0.0).reshape(256, 128).astype(BF16)
-
-    def translate(c):
+        return jnp.where(iota(shape, 2) < 121, rows, 0.0).reshape(8 * n, 128).astype(BF16)
+
+    def translate(c, beside):
         q0, n = CHUNKS[c]
-        total = jnp.zeros((256, 128), F32)
-        for j in range(0, 49, 2):
+        n += n % 2
+        total = jnp.zeros((8 * n, 128), F32)
+        for step in range(STEPS):
+            j = 2 * step
+            w = weights(q0, n, j)
+            width = 128
             if j + 1 < 49:
-                w = jnp.concatenate([weights(q0, j), weights(q0, j + 1)], axis=1)
-                total = total + lax.dot_general(w, G[:, 128 * j:128 * j + 256], NT, preferred_element_type=F32)
-            else:
-                total = total + lax.dot_general(
-                    weights(q0, j), G[:, 128 * j:128 * j + 128], NT, preferred_element_type=F32)
-        total = total.reshape(cell)
-        skewed = pltpu.roll(total, 0, 2, stride=1, stride_axis=1)
+                w = jnp.concatenate([w, weights(q0, n, j + 1)], axis=1)
+                width = 256
+            total = total + lax.dot_general(w, G[:, 128 * j:128 * j + width], NT, preferred_element_type=F32)
+            beside(step)
+        return total
+
+    def settle(c, total):
+        q0, n = CHUNKS[c]
+        rows = n + n % 2
+        cell = (rows, 8, 128)
+        dz = iota(cell, 1) - 3
+        source_z = (iota(cell, 2) & 7) - dz
+        inside = (source_z >= 0) & (source_z <= 7)
+        odd_z = (iota(cell, 2) & 1) == 0
+        valid = (jnp.abs(dz) < 3) | ((dz == -3) & odd_z) | ((dz == 3) & jnp.logical_not(odd_z))
+        skewed = pltpu.roll(total.reshape(cell), 0, 2, stride=1, stride_axis=1)
         turned = pltpu.roll(skewed, 125, 2)
         wrapped = jnp.where(dz > 0, pltpu.roll(skewed, 117, 2), pltpu.roll(skewed, 5, 2))
         picked = jnp.where(valid, jnp.where(inside, turned, wrapped), 0.0)
         sums = jnp.sum(picked, axis=1, keepdims=True)
-        wide = jnp.broadcast_to(sums, cell).reshape(16, 2, 8, 128)
-        wide = jnp.where(iota((16, 8, 128), 1) < 4, wide[:, 0], wide[:, 1]).reshape(128, 128)
-        if n < 32:
-            wide = jnp.where(iota((128, 128), 0) < 4 * n, wide, 0.0)
-        Lrep[4 * q0:4 * q0 + 128, :] = wide.astype(BF16)
+        wide = jnp.broadcast_to(sums, cell).reshape(rows // 2, 2, 8, 128)
+        wide = jnp.where(iota((rows // 2, 8, 128), 1) < 4, wide[:, 0], wide[:, 1]).reshape(4 * rows, 128)
+        if n < rows:
+            wide = jnp.where(iota((4 * rows, 128), 0) < 4 * n, wide, 0.0)
+            Lrep[4 * (q0 + rows):496, :] = jnp.zeros((496 - 4 * (q0 + rows), 128), BF16)
+        Lrep[4 * q0:4 * (q0 + rows), :] = wide.astype(BF16)
         return jnp.sum(picked, axis=1)
 
     def put_local(c, sums):
         q0, n = CHUNKS[c]
         local_out[q0:q0 + n, :] = mirror_z(sums)[0:n].astype(BF16)
 
-    F[121:128] = jnp.zeros((7, 320, 128), F32)
+    F[121:122] = jnp.zeros((1, 320, 128), F32)
+    done = None
     for c in range(3):
-        if c:
-            widen(c)
-        put_local(c, translate(c))
-    widen(3)
+        op_loads[c + 1].wait()
+
+        def beside(step):
+            widen(c + 1, step)
+            if step == 4 and done is not None:
+                put_local(c - 1, settle(c - 1, done))
+
+        done = translate(c, beside)
 
     for g in range(8):
         guests[g].wait_recv()
@@ -240,7 +255,11 @@
     guest_slot = Ef[488:489, 2048:2304].astype(jnp.int32) ^ 7
     OH[:, 2048:2304] = one_hot(iota((128, 256), 0) == guest_slot)
 
-    last = translate(3)
+    def beside_last(step):
+        if step == 4:
+            put_local(2, settle(2, done))
+
+    last = settle(3, translate(3, beside_last))
 
     def evaluate(start):
         values = lax.dot_general(
@@ -300,23 +319,33 @@
         answers[g].wait_send()
 
 
+def hand_on(*refs):
+    sem = refs[-1]
+    copies = [pltpu.make_async_copy(refs[i], refs[3 + i], sem.at[i]) for i in range(3)]
+    for copy in copies:
+        copy.start()
+    for copy in copies:
+        copy.wait()
+
+
 def shards(mult, ops, table, ev, ions, owner, slot):
     nx, ny = lax.axis_size("xs"), lax.axis_size("ys")
     dma = pltpu.SemaphoreType.DMA
     vmem = pltpu.VMEM
-    return pl.pallas_call(
+    outs = (
+        jax.ShapeDtypeStruct((121, 128), BF16),
+        jax.ShapeDtypeStruct((4, 2048), F32),
+        jax.ShapeDtypeStruct((9, 128), F32),
+    )
+    found = pl.pallas_call(
         functools.partial(kernel, nx, ny),
-        out_shape=(
-            jax.ShapeDtypeStruct((121, 128), BF16),
-            jax.ShapeDtypeStruct((4, 2048), F32),
-            jax.ShapeDtypeStruct((9, 128), F32),
-        ),
+        out_shape=outs,
         in_specs=[pl.BlockSpec(memory_space=pl.ANY)] * 7,
         out_specs=[pl.BlockSpec(memory_space=pltpu.VMEM)] * 3,
         scratch_shapes=[
             vmem((121, 128), BF16), vmem((8, 128), jnp.int32), vmem((4, 2048), BF16),
             vmem((1, 2048), jnp.int32), vmem((1, 2048), jnp.int32),
-            vmem((121, 4, 2048), BF16), vmem((121, 316, 121), BF16), vmem((128, 320, 128), F32),
+            vmem((121, 4, 2048), BF16), vmem((121, 316, 121), BF16), vmem((122, 320, 128), F32),
             vmem((512, 2304), F32), vmem((256, 2048), BF16), vmem((128, 2304), BF16),
             vmem((10, 10, 8, 128), F32), vmem((128, 49 * 128), BF16),
             vmem((128, 128), BF16), vmem((8, 128, 128), BF16), vmem((256, 512), BF16), vmem((256, 512), BF16),
@@ -334,6 +363,13 @@
         jnp.reshape(owner, (1, owner.shape[0])),
         jnp.reshape(slot, (1, slot.shape[0])),
     )
+    return pl.pallas_call(
+        hand_on,
+        out_shape=outs,
+        in_specs=[pl.BlockSpec(memory_space=pl.ANY)] * 3,
+        out_specs=[pl.BlockSpec(memory_space=pl.ANY)] * 3,
+        scratch_shapes=[dma((3,))],
+    )(*found)
 
 
 def solution(mesh):

time: 35 us -> 33 us (0.943)
  local copies, waits for them, and re-layouts: 4.04 us -> 0 us
  Pallas kernels: 30 us -> 32.2 us
    unnamed x3 -> x0, local copies, waits for them, and re-layouts: 4.04 us -> none
    pallas_call x1 -> x2, Pallas kernels: 30 us -> 32.2 us  [the longest x1 29 us: shards(): pl.pallas_call(functools.partial(kernel, nx, ny), out_shape=outs, in_spec...]
where the time goes in v2:
time: 33 us; the launch traced here: 32.9 us
  Pallas kernels  32.2 us (98%)
  between operations  0.64 us (2%)
    pallas_call x1, Pallas kernels, shards(): pl.pallas_call(functools.partial(kernel, nx, ny), out_shape=outs, in_spec...  29 us
    pallas_call x1, Pallas kernels, shards(): pl.pallas_call(hand_on, out_shape=outs, in_specs=[pl.BlockSpec(memory_spa...  3.26 us

profile of v2, /device:TPU:0, one launch (start us, length us, event | category | flops | bytes accessed | tf_op | source)
XLA Modules:
  0.0 32.9 jit_solution(1037416633515510711)
XLA Ops:
  0.6 29.0 %shard_map.94 = (bf16[121,128]{1,0:T(8,128)(2,1)}, f32[4,2048]{1,0:T(4,128)}, f32[9,128]{1,0:T(8,128)}) custom-call(bf16[121,128]{1,0:T(8,128)(2,1)} %mult.1, bf16[121,316,121]{2,1,0:T(8,128)(2,1)} %bitcast.4, s32[316,128]{1,0:T(8,128)} %table.1, bf16[121,4,2048]{2,1,0:T(4,128)(2,1)} %bitcast.5, bf16[4,2048]{1,0:T(4,128)(2,1)} %ions.1, s32[1,2048]{1,0:T(1,128)} %bitcast.6, ...), custom_call_target="tpu_custom_call" | custom-call | tf_op jit(solution)/shard_map/pallas_call | solution.py:340
  29.6 3.3 %shard_map.95 = (bf16[121,128]{1,0:T(8,128)(2,1)}, f32[4,2048]{1,0:T(4,128)}, f32[9,128]{1,0:T(8,128)}) custom-call(bf16[121,128]{1,0:T(8,128)(2,1)} %get-tuple-element.6.refs_0_, f32[4,2048]{1,0:T(4,128)} %get-tuple-element.7.refs_1_, f32[9,128]{1,0:T(8,128)} %get-tuple-element.8.refs_2_), custom_call_target="tpu_custom_call" | custom-call | tf_op jit(solution)/shard_map/pallas_call | solution.py:366

commit v3 on v2

--- a/solution.py
+++ b/solution.py
@@ -26,10 +26,11 @@
     return listed
 
 
-COLUMNS = offset_columns()
+COLUMNS = sorted(offset_columns(), key=lambda c: 2 if c[3] else c[2] % 2)
+GROUP = [2 if c[3] else c[2] % 2 for c in COLUMNS]
+SPANS = [(GROUP.index(g), GROUP.index(g) + GROUP.count(g)) for g in range(3)]
 SELF_ROW = [c[2] for c in COLUMNS if c[:2] == (0, 0)][0] + 1
 CHUNKS = [(0, 32), (32, 32), (64, 32), (96, 25)]
-STEPS = 25
 
 
 def iota(shape, axis):
@@ -52,7 +53,7 @@
     nx, ny,
     mult, ops, table, ev, ions, owner, slot,
     local_out, field_out, virial_out,
-    mraw, trow, iraw, oraw, sraw, eb, tb, F, Ef, R, OH, ext, G,
+    mraw, trow, iraw, oraw, sraw, eb, tb, Ef, R, OH, ext, G,
     msend, mrecv, ec, gmsg, fg, ret, Lrep, fo,
     in_sem, op_sem, s1, r1, s2, r2, s3, r3,
 ):
@@ -78,15 +79,14 @@
         pltpu.make_async_copy(ops.at[pl.ds(q0, n)], tb.at[pl.ds(q0, n)], op_sem.at[c])
         for c, (q0, n) in enumerate(CHUNKS)
     ]
+    barrier = pltpu.get_barrier_semaphore()
+    for g in range(8):
+        pl.semaphore_signal(barrier, inc=1, device_id=peer(g), device_id_type=MESH)
+
+    loads[0].wait()
+    loads[1].wait()
     for copy in op_loads:
         copy.start()
-
-    barrier = pltpu.get_barrier_semaphore()
-    for g in range(8):
-        pl.semaphore_signal(barrier, inc=1, device_id=peer(g), device_id_type=MESH)
-
-    loads[0].wait()
-    loads[1].wait()
     named = trow[SELF_ROW - first:SELF_ROW - first + 1, :]
     lane = iota((1, 128), 1)
     named = jnp.where((lane & 7) < 6, pltpu.roll(named, 126, 1), pltpu.roll(named, 6, 1))
@@ -156,15 +156,6 @@
             device_id=peer(7 - g), device_id_type=MESH))
         guests[-1].start()
 
-    def widen(c, step):
-        q0, n = CHUNKS[c]
-        low, high = q0 + n * step // STEPS, q0 + n * (step + 1) // STEPS
-        F[low:high, 0:316, 0:121] = tb[low:high].astype(F32)
-
-    op_loads[0].wait()
-    for step in range(STEPS):
-        widen(0, step)
-
     def place_block(block, ex, ey):
         block = block.astype(F32).reshape(4, 4, 8, 128)
         sx = {-1: (1, 4, 0), 0: (0, 4, 3), 1: (0, 3, 7)}[ex]
@@ -185,67 +176,67 @@
         G[:, 128 * j:128 * j + 128] = block.reshape(128, 128).astype(BF16)
 
     def weights(q0, n, j):
-        _, _, k0, near = COLUMNS[j]
-        shape = (n, 8, 128)
-        rows = F[q0:q0 + n, k0:k0 + 8, :]
-        if near:
-            slots = iota(shape, 1)
-            upper = F[q0:q0 + n, k0 - 3:k0 + 5, :]
-            rows = jnp.where(slots < 2, rows, jnp.where((slots >= 5) & (slots < 7), upper, 0.0))
-        return jnp.where(iota(shape, 2) < 121, rows, 0.0).reshape(8 * n, 128).astype(BF16)
+        k0 = COLUMNS[j][2] // 2 * 2
+        rows = tb[q0:q0 + n, k0:k0 + 8, :].reshape(8 * n, 121)
+        return jnp.concatenate([rows, jnp.zeros((8 * n, 7), BF16)], axis=1)
 
     def translate(c, beside):
         q0, n = CHUNKS[c]
-        n += n % 2
-        total = jnp.zeros((8 * n, 128), F32)
-        for step in range(STEPS):
-            j = 2 * step
-            w = weights(q0, n, j)
-            width = 128
-            if j + 1 < 49:
-                w = jnp.concatenate([w, weights(q0, n, j + 1)], axis=1)
-                width = 256
-            total = total + lax.dot_general(w, G[:, 128 * j:128 * j + width], NT, preferred_element_type=F32)
-            beside(step)
-        return total
-
-    def settle(c, total):
+        q0, n = q0 - n % 2, n + n % 2
+        totals, step = [], 0
+        for low, high in SPANS:
+            total = jnp.zeros((8 * n, 128), F32)
+            for j in range(low, high, 2):
+                w = weights(q0, n, j)
+                width = 128
+                if j + 1 < high:
+                    w = jnp.concatenate([w, weights(q0, n, j + 1)], axis=1)
+                    width = 256
+                total = total + lax.dot_general(
+                    w, G[:, 128 * j:128 * j + width], NT, preferred_element_type=F32)
+                step += 1
+                if step == 4:
+                    beside()
+            totals.append(total.reshape(n, 8, 128))
+        return totals
+
+    def settle(c, totals):
         q0, n = CHUNKS[c]
-        rows = n + n % 2
+        rows = (n + 3) // 4 * 4
+        if n % 2:
+            totals = [jnp.concatenate([t[1:], jnp.zeros((rows - n, 8, 128), F32)], axis=0) for t in totals]
         cell = (rows, 8, 128)
-        dz = iota(cell, 1) - 3
+        at = iota(cell, 1)
+        even, odd, near = totals
+        total = even + pltpu.roll(odd, 7, 1)
+        total = total + jnp.where(at < 2, near, jnp.where((at == 5) | (at == 6), pltpu.roll(near, 3, 1), 0.0))
+        dz = at - 3
         source_z = (iota(cell, 2) & 7) - dz
         inside = (source_z >= 0) & (source_z <= 7)
         odd_z = (iota(cell, 2) & 1) == 0
         valid = (jnp.abs(dz) < 3) | ((dz == -3) & odd_z) | ((dz == 3) & jnp.logical_not(odd_z))
-        skewed = pltpu.roll(total.reshape(cell), 0, 2, stride=1, stride_axis=1)
+        skewed = pltpu.roll(total, 0, 2, stride=1, stride_axis=1)
         turned = pltpu.roll(skewed, 125, 2)
         wrapped = jnp.where(dz > 0, pltpu.roll(skewed, 117, 2), pltpu.roll(skewed, 5, 2))
         picked = jnp.where(valid, jnp.where(inside, turned, wrapped), 0.0)
         sums = jnp.sum(picked, axis=1, keepdims=True)
         wide = jnp.broadcast_to(sums, cell).reshape(rows // 2, 2, 8, 128)
         wide = jnp.where(iota((rows // 2, 8, 128), 1) < 4, wide[:, 0], wide[:, 1]).reshape(4 * rows, 128)
-        if n < rows:
-            wide = jnp.where(iota((4 * rows, 128), 0) < 4 * n, wide, 0.0)
-            Lrep[4 * (q0 + rows):496, :] = jnp.zeros((496 - 4 * (q0 + rows), 128), BF16)
-        Lrep[4 * q0:4 * (q0 + rows), :] = wide.astype(BF16)
-        return jnp.sum(picked, axis=1)
+        Lrep[4 * q0:4 * q0 + 4 * rows, :] = wide.astype(BF16)
+        return sums.reshape(rows, 128)
 
     def put_local(c, sums):
         q0, n = CHUNKS[c]
         local_out[q0:q0 + n, :] = mirror_z(sums)[0:n].astype(BF16)
 
-    F[121:122] = jnp.zeros((1, 320, 128), F32)
-    done = None
-    for c in range(3):
-        op_loads[c + 1].wait()
-
-        def beside(step):
-            widen(c + 1, step)
-            if step == 4 and done is not None:
-                put_local(c - 1, settle(c - 1, done))
-
-        done = translate(c, beside)
+    assert all(c[2] % 2 == 0 for c in COLUMNS if c[3])
+    op_loads[0].wait()
+    done = translate(0, lambda: None)
+    op_loads[1].wait()
+    op_loads[2].wait()
+    for c in (1, 2):
+        before_it = done
+        done = translate(c, lambda: put_local(c - 1, settle(c - 1, before_it)))
 
     for g in range(8):
         guests[g].wait_recv()
@@ -255,11 +246,8 @@
     guest_slot = Ef[488:489, 2048:2304].astype(jnp.int32) ^ 7
     OH[:, 2048:2304] = one_hot(iota((128, 256), 0) == guest_slot)
 
-    def beside_last(step):
-        if step == 4:
-            put_local(2, settle(2, done))
-
-    last = settle(3, translate(3, beside_last))
+    op_loads[3].wait()
+    last = settle(3, translate(3, lambda: put_local(2, settle(2, done))))
 
     def evaluate(start):
         values = lax.dot_general(
@@ -339,13 +327,13 @@
     )
     found = pl.pallas_call(
         functools.partial(kernel, nx, ny),
-        out_shape=outs,
+        out_shape=(vmem((121, 128), BF16), vmem((4, 2048), F32), vmem((9, 128), F32)),
         in_specs=[pl.BlockSpec(memory_space=pl.ANY)] * 7,
         out_specs=[pl.BlockSpec(memory_space=pltpu.VMEM)] * 3,
         scratch_shapes=[
             vmem((121, 128), BF16), vmem((8, 128), jnp.int32), vmem((4, 2048), BF16),
             vmem((1, 2048), jnp.int32), vmem((1, 2048), jnp.int32),
-            vmem((121, 4, 2048), BF16), vmem((121, 316, 121), BF16), vmem((122, 320, 128), F32),
+            vmem((121, 4, 2048), BF16), vmem((121, 316, 121), BF16),
             vmem((512, 2304), F32), vmem((256, 2048), BF16), vmem((128, 2304), BF16),
             vmem((10, 10, 8, 128), F32), vmem((128, 49 * 128), BF16),
             vmem((128, 128), BF16), vmem((8, 128, 128), BF16), vmem((256, 512), BF16), vmem((256, 512), BF16),
@@ -366,10 +354,10 @@
     return pl.pallas_call(
         hand_on,
         out_shape=outs,
-        in_specs=[pl.BlockSpec(memory_space=pl.ANY)] * 3,
+        in_specs=[pl.BlockSpec(memory_space=pltpu.VMEM)] * 3,
         out_specs=[pl.BlockSpec(memory_space=pl.ANY)] * 3,
         scratch_shapes=[dma((3,))],
-    )(*found)
+    )(*[pltpu.with_memory_space_constraint(x, pltpu.VMEM) for x in found])
 
 
 def solution(mesh):

time: 33 us -> 27.1 us (0.82)
  Pallas kernels: 32.2 us -> 26.3 us
    pallas_call x1, Pallas kernels: 29 us -> 25.7 us  [shards(): pl.pallas_call(functools.partial(kernel, nx, ny), out_shape=(vmem((121, 1...]
    pallas_call x1, Pallas kernels: 3.26 us -> 0.66 us  [shards(): pl.pallas_call(hand_on, out_shape=outs, in_specs=[pl.BlockSpec(memory_spa...]
where the time goes in v3:
time: 27.1 us; the launch traced here: 27 us
  Pallas kernels  26.3 us (97%)
  between operations  0.64 us (2%)
    pallas_call x1, Pallas kernels, shards(): pl.pallas_call(functools.partial(kernel, nx, ny), out_shape=(vmem((121, 1...  25.7 us
    pallas_call x1, Pallas kernels, shards(): pl.pallas_call(hand_on, out_shape=outs, in_specs=[pl.BlockSpec(memory_spa...  0.66 us

profile of v3, /device:TPU:0, one launch (start us, length us, event | category | flops | bytes accessed | tf_op | source)
XLA Modules:
  0.0 27.0 jit_solution(10866804869224067601)
XLA Ops:
  0.6 25.7 %shard_map.94 = (bf16[121,128]{1,0:T(8,128)(2,1)S(1)}, f32[4,2048]{1,0:T(4,128)S(1)}, f32[9,128]{1,0:T(8,128)S(1)}) custom-call(bf16[121,128]{1,0:T(8,128)(2,1)} %mult.1, bf16[121,316,121]{2,1,0:T(8,128)(2,1)} %bitcast.4, s32[316,128]{1,0:T(8,128)} %table.1, bf16[121,4,2048]{2,1,0:T(4,128)(2,1)} %bitcast.5, bf16[4,2048]{1,0:T(4,128)(2,1)} %ions.1, ...), custom_call_target="tpu_custom_call" | custom-call | tf_op jit(solution)/shard_map/pallas_call | solution.py:328
  26.3 0.7 %shard_map.95 = (bf16[121,128]{1,0:T(8,128)(2,1)}, f32[4,2048]{1,0:T(4,128)}, f32[9,128]{1,0:T(8,128)}) custom-call(bf16[121,128]{1,0:T(8,128)(2,1)S(1)} %get-tuple-element.6.refs_0_, f32[4,2048]{1,0:T(4,128)S(1)} %get-tuple-element.7.refs_1_, f32[9,128]{1,0:T(8,128)S(1)} %get-tuple-element.8.refs_2_), custom_call_target="tpu_custom_call" | custom-call | tf_op jit(solution)/shard_map/pallas_call | solution.py:354

commit v4 on v3

--- a/solution.py
+++ b/solution.py
@@ -14,6 +14,7 @@
 BF16 = jnp.bfloat16
 
 AROUND = [(ex, ey) for ex in (-1, 0, 1) for ey in (-1, 0, 1) if (ex, ey) != (0, 0)]
+FAR_FIRST = (0, 2, 5, 7, 1, 6, 3, 4)
 
 
 def offset_columns():
@@ -73,16 +74,18 @@
         pltpu.make_async_copy(ions, iraw, in_sem.at[4]),
         pltpu.make_async_copy(ev, eb, in_sem.at[5]),
     ]
-    for copy in loads:
+    for copy in loads[:2]:
+        copy.start()
+    barrier = pltpu.get_barrier_semaphore()
+    for g in FAR_FIRST:
+        pl.semaphore_signal(barrier, inc=1, device_id=peer(g), device_id_type=MESH)
+
+    for copy in loads[2:]:
         copy.start()
     op_loads = [
         pltpu.make_async_copy(ops.at[pl.ds(q0, n)], tb.at[pl.ds(q0, n)], op_sem.at[c])
         for c, (q0, n) in enumerate(CHUNKS)
     ]
-    barrier = pltpu.get_barrier_semaphore()
-    for g in range(8):
-        pl.semaphore_signal(barrier, inc=1, device_id=peer(g), device_id_type=MESH)
-
     loads[0].wait()
     loads[1].wait()
     for copy in op_loads:
@@ -97,14 +100,14 @@
     msend[:, 0:121] = turned.astype(BF16)
 
     pl.semaphore_wait(barrier, 8)
-    halo = []
-    for g in range(8):
+    halo = [None] * 8
+    for g in FAR_FIRST:
         ex = AROUND[g][0]
-        rows = pl.ds(32 if ex < 0 else 0, 128 if ex == 0 else 96)
-        halo.append(pltpu.make_async_remote_copy(
+        rows = pl.ds(64 if ex < 0 else 0, 128 if ex == 0 else 64)
+        halo[g] = pltpu.make_async_remote_copy(
             src_ref=msend.at[rows], dst_ref=mrecv.at[g, rows], send_sem=s1.at[g], recv_sem=r1.at[g],
-            device_id=peer(7 - g), device_id_type=MESH))
-        halo[-1].start()
+            device_id=peer(7 - g), device_id_type=MESH)
+        halo[g].start()
 
     loads[2].wait()
     loads[3].wait()
@@ -148,22 +151,24 @@
 
     ec[...] = lax.dot_general(
         R[...], Ef[:, 0:2048].astype(BF16), NT, preferred_element_type=F32).astype(BF16)
-    guests = []
-    for g in range(8):
+    guests = [None] * 8
+    for g in FAR_FIRST:
         rows = pl.ds(32 * g, 32)
-        guests.append(pltpu.make_async_remote_copy(
+        guests[g] = pltpu.make_async_remote_copy(
             src_ref=ec.at[rows], dst_ref=gmsg.at[rows], send_sem=s2.at[g], recv_sem=r2.at[g],
-            device_id=peer(7 - g), device_id_type=MESH))
-        guests[-1].start()
+            device_id=peer(7 - g), device_id_type=MESH)
+        guests[g].start()
 
     def place_block(block, ex, ey):
         block = block.astype(F32).reshape(4, 4, 8, 128)
-        sx = {-1: (1, 4, 0), 0: (0, 4, 3), 1: (0, 3, 7)}[ex]
-        sy = {-1: (1, 4, 0), 0: (0, 4, 3), 1: (0, 3, 7)}[ey]
+        sx = {-1: (2, 4, 1), 0: (0, 4, 3), 1: (0, 2, 7)}[ex]
+        sy = {-1: (2, 4, 1), 0: (0, 4, 3), 1: (0, 2, 7)}[ey]
         ext[sx[2]:sx[2] + sx[1] - sx[0], sy[2]:sy[2] + sy[1] - sy[0]] = block[sx[0]:sx[1], sy[0]:sy[1]]
 
     place_block(msend[...], 0, 0)
-    for g in range(8):
+    for copy in op_loads:
+        copy.wait()
+    for g in (3, 4, 1, 6, 0, 2, 5, 7):
         halo[g].wait_recv()
         place_block(mrecv[g], *AROUND[g])
     grid_x, grid_y = iota((4, 4, 8, 128), 0), iota((4, 4, 8, 128), 1)
@@ -230,10 +235,7 @@
         local_out[q0:q0 + n, :] = mirror_z(sums)[0:n].astype(BF16)
 
     assert all(c[2] % 2 == 0 for c in COLUMNS if c[3])
-    op_loads[0].wait()
     done = translate(0, lambda: None)
-    op_loads[1].wait()
-    op_loads[2].wait()
     for c in (1, 2):
         before_it = done
         done = translate(c, lambda: put_local(c - 1, settle(c - 1, before_it)))
@@ -246,7 +248,6 @@
     guest_slot = Ef[488:489, 2048:2304].astype(jnp.int32) ^ 7
     OH[:, 2048:2304] = one_hot(iota((128, 256), 0) == guest_slot)
 
-    op_loads[3].wait()
     last = settle(3, translate(3, lambda: put_local(2, settle(2, done))))
 
     def evaluate(start):
@@ -260,12 +261,12 @@
     fo[:, 2048:2304] = far
     fg[0] = far[:, 0:128]
     fg[1] = far[:, 128:256]
-    answers = []
-    for g in range(8):
-        answers.append(pltpu.make_async_remote_copy(
+    answers = [None] * 8
+    for g in FAR_FIRST:
+        answers[g] = pltpu.make_async_remote_copy(
             src_ref=fg.at[g // 4], dst_ref=ret.at[g], send_sem=s3.at[g], recv_sem=r3.at[g],
-            device_id=peer(g), device_id_type=MESH))
-        answers[-1].start()
+            device_id=peer(g), device_id_type=MESH)
+        answers[g].start()
     put_local(3, last)
     for b in range(8):
         fo[:, 256 * b:256 * b + 256] = evaluate(256 * b)

time: 27.1 us -> 25.6 us (0.945)
  Pallas kernels: 26.3 us -> 24.9 us
    pallas_call x1, Pallas kernels: 25.7 us -> 24.2 us  [shards(): pl.pallas_call(functools.partial(kernel, nx, ny), out_shape=(vmem((121, 1...]
where the time goes in v4:
time: 25.6 us; the launch traced here: 25.5 us
  Pallas kernels  24.9 us (97%)
  between operations  0.64 us (2%)
    pallas_call x1, Pallas kernels, shards(): pl.pallas_call(functools.partial(kernel, nx, ny), out_shape=(vmem((121, 1...  24.2 us
    pallas_call x1, Pallas kernels, shards(): pl.pallas_call(hand_on, out_shape=outs, in_specs=[pl.BlockSpec(memory_spa...  0.66 us

profile of v4, /device:TPU:0, one launch (start us, length us, event | category | flops | bytes accessed | tf_op | source)
XLA Modules:
  0.0 25.5 jit_solution(12723319314819529039)
XLA Ops:
  0.6 24.2 %shard_map.94 = (bf16[121,128]{1,0:T(8,128)(2,1)S(1)}, f32[4,2048]{1,0:T(4,128)S(1)}, f32[9,128]{1,0:T(8,128)S(1)}) custom-call(bf16[121,128]{1,0:T(8,128)(2,1)} %mult.1, bf16[121,316,121]{2,1,0:T(8,128)(2,1)} %bitcast.4, s32[316,128]{1,0:T(8,128)} %table.1, bf16[121,4,2048]{2,1,0:T(4,128)(2,1)} %bitcast.5, bf16[4,2048]{1,0:T(4,128)(2,1)} %ions.1, ...), custom_call_target="tpu_custom_call" | custom-call | tf_op jit(solution)/shard_map/pallas_call | solution.py:329
  24.8 0.7 %shard_map.95 = (bf16[121,128]{1,0:T(8,128)(2,1)}, f32[4,2048]{1,0:T(4,128)}, f32[9,128]{1,0:T(8,128)}) custom-call(bf16[121,128]{1,0:T(8,128)(2,1)S(1)} %get-tuple-element.6.refs_0_, f32[4,2048]{1,0:T(4,128)S(1)} %get-tuple-element.7.refs_1_, f32[9,128]{1,0:T(8,128)S(1)} %get-tuple-element.8.refs_2_), custom_call_target="tpu_custom_call" | custom-call | tf_op jit(solution)/shard_map/pallas_call | solution.py:355

commit v5 on v4

--- a/solution.py
+++ b/solution.py
@@ -27,9 +27,15 @@
     return listed
 
 
-COLUMNS = sorted(offset_columns(), key=lambda c: 2 if c[3] else c[2] % 2)
-GROUP = [2 if c[3] else c[2] % 2 for c in COLUMNS]
-SPANS = [(GROUP.index(g), GROUP.index(g) + GROUP.count(g)) for g in range(3)]
+def sort_key(column):
+    dx, dy, row, near = column
+    return (0 if dx == 0 or dy == 0 else 1, 2 if near else row % 2)
+
+
+COLUMNS = sorted(offset_columns(), key=sort_key)
+GROUP = [sort_key(c) for c in COLUMNS]
+SPANS = [[(GROUP.index((s, g)), GROUP.index((s, g)) + GROUP.count((s, g))) for g in range(3)] for s in range(2)]
+STRAIGHT = SPANS[1][0][0]
 SELF_ROW = [c[2] for c in COLUMNS if c[:2] == (0, 0)][0] + 1
 CHUNKS = [(0, 32), (32, 32), (64, 32), (96, 25)]
 
@@ -55,7 +61,7 @@
     mult, ops, table, ev, ions, owner, slot,
     local_out, field_out, virial_out,
     mraw, trow, iraw, oraw, sraw, eb, tb, Ef, R, OH, ext, G,
-    msend, mrecv, ec, gmsg, fg, ret, Lrep, fo,
+    part, msend, mrecv, ec, gmsg, fg, ret, Lrep, fo,
     in_sem, op_sem, s1, r1, s2, r2, s3, r3,
 ):
     mx = lax.axis_index("xs")
@@ -168,11 +174,13 @@
     place_block(msend[...], 0, 0)
     for copy in op_loads:
         copy.wait()
-    for g in (3, 4, 1, 6, 0, 2, 5, 7):
+    for g in (3, 4, 1, 6):
         halo[g].wait_recv()
         place_block(mrecv[g], *AROUND[g])
     grid_x, grid_y = iota((4, 4, 8, 128), 0), iota((4, 4, 8, 128), 1)
-    for j, (dx, dy, _, _) in enumerate(COLUMNS):
+
+    def gather(j):
+        dx, dy, _, _ = COLUMNS[j]
         block = ext[dx + 3:dx + 7, dy + 3:dy + 7]
         if abs(dx) == 3:
             block = jnp.where((grid_x & 1) == (0 if dx > 0 else 1), block, 0.0)
@@ -180,17 +188,20 @@
             block = jnp.where((grid_y & 1) == (0 if dy > 0 else 1), block, 0.0)
         G[:, 128 * j:128 * j + 128] = block.reshape(128, 128).astype(BF16)
 
+    for j in range(STRAIGHT):
+        gather(j)
+
     def weights(q0, n, j):
         k0 = COLUMNS[j][2] // 2 * 2
         rows = tb[q0:q0 + n, k0:k0 + 8, :].reshape(8 * n, 121)
         return jnp.concatenate([rows, jnp.zeros((8 * n, 7), BF16)], axis=1)
 
-    def translate(c, beside):
+    def translate(stage, c, totals, beside):
         q0, n = CHUNKS[c]
         q0, n = q0 - n % 2, n + n % 2
-        totals, step = [], 0
-        for low, high in SPANS:
-            total = jnp.zeros((8 * n, 128), F32)
+        step = 0
+        for group, (low, high) in enumerate(SPANS[stage]):
+            total = totals[group]
             for j in range(low, high, 2):
                 w = weights(q0, n, j)
                 width = 128
@@ -202,8 +213,23 @@
                 step += 1
                 if step == 4:
                     beside()
-            totals.append(total.reshape(n, 8, 128))
+            totals[group] = total
         return totals
+
+    def finish(c, beside):
+        n = CHUNKS[c][1] + CHUNKS[c][1] % 2
+        totals = translate(1, c, [part[c, group, 0:8 * n, :] for group in range(3)], beside)
+        return [total.reshape(n, 8, 128) for total in totals]
+
+    for c in range(4):
+        n = CHUNKS[c][1] + CHUNKS[c][1] % 2
+        for group, total in enumerate(translate(0, c, [jnp.zeros((8 * n, 128), F32)] * 3, lambda: None)):
+            part[c, group, 0:8 * n, :] = total
+    for g in (0, 2, 5, 7):
+        halo[g].wait_recv()
+        place_block(mrecv[g], *AROUND[g])
+    for j in range(STRAIGHT, 49):
+        gather(j)
 
     def settle(c, totals):
         q0, n = CHUNKS[c]
@@ -235,10 +261,10 @@
         local_out[q0:q0 + n, :] = mirror_z(sums)[0:n].astype(BF16)
 
     assert all(c[2] % 2 == 0 for c in COLUMNS if c[3])
-    done = translate(0, lambda: None)
+    done = finish(0, lambda: None)
     for c in (1, 2):
         before_it = done
-        done = translate(c, lambda: put_local(c - 1, settle(c - 1, before_it)))
+        done = finish(c, lambda: put_local(c - 1, settle(c - 1, before_it)))
 
     for g in range(8):
         guests[g].wait_recv()
@@ -248,7 +274,7 @@
     guest_slot = Ef[488:489, 2048:2304].astype(jnp.int32) ^ 7
     OH[:, 2048:2304] = one_hot(iota((128, 256), 0) == guest_slot)
 
-    last = settle(3, translate(3, lambda: put_local(2, settle(2, done))))
+    last = settle(3, finish(3, lambda: put_local(2, settle(2, done))))
 
     def evaluate(start):
         values = lax.dot_general(
@@ -336,7 +362,7 @@
             vmem((1, 2048), jnp.int32), vmem((1, 2048), jnp.int32),
             vmem((121, 4, 2048), BF16), vmem((121, 316, 121), BF16),
             vmem((512, 2304), F32), vmem((256, 2048), BF16), vmem((128, 2304), BF16),
-            vmem((10, 10, 8, 128), F32), vmem((128, 49 * 128), BF16),
+            vmem((10, 10, 8, 128), F32), vmem((128, 49 * 128), BF16), vmem((4, 3, 256, 128), F32),
             vmem((128, 128), BF16), vmem((8, 128, 128), BF16), vmem((256, 512), BF16), vmem((256, 512), BF16),
             vmem((2, 8, 128), F32), vmem((8, 8, 128), F32), vmem((512, 128), BF16), vmem((8, 2304), F32),
             dma((6,)), dma((4,)), dma((8,)), dma((8,)), dma((8,)), dma((8,)), dma((8,)), dma((8,)),

time: 25.6 us -> 25.9 us (1.012)
  the two profiles are of different devices: /device:TPU:0 before, /device:TPU:1 now
where the time goes in v5:
time: 25.9 us; the launch traced here: 25.8 us
  Pallas kernels  25.1 us (97%)
  between operations  0.64 us (2%)
    pallas_call x1, Pallas kernels, shards(): pl.pallas_call(functools.partial(kernel, nx, ny), out_shape=(vmem((121, 1...  24.5 us
    pallas_call x1, Pallas kernels, shards(): pl.pallas_call(hand_on, out_shape=outs, in_specs=[pl.BlockSpec(memory_spa...  0.66 us

profile of v5, /device:TPU:1, one launch (start us, length us, event | category | flops | bytes accessed | tf_op | source)
XLA Modules:
  0.0 25.8 jit_solution(3898221384568986536)
XLA Ops:
  0.6 24.5 %shard_map.94 = (bf16[121,128]{1,0:T(8,128)(2,1)S(1)}, f32[4,2048]{1,0:T(4,128)S(1)}, f32[9,128]{1,0:T(8,128)S(1)}) custom-call(bf16[121,128]{1,0:T(8,128)(2,1)} %mult.1, bf16[121,316,121]{2,1,0:T(8,128)(2,1)} %bitcast.4, s32[316,128]{1,0:T(8,128)} %table.1, bf16[121,4,2048]{2,1,0:T(4,128)(2,1)} %bitcast.5, bf16[4,2048]{1,0:T(4,128)(2,1)} %ions.1, ...), custom_call_target="tpu_custom_call" | custom-call | tf_op jit(solution)/shard_map/pallas_call | solution.py:355
  25.1 0.7 %shard_map.95 = (bf16[121,128]{1,0:T(8,128)(2,1)}, f32[4,2048]{1,0:T(4,128)}, f32[9,128]{1,0:T(8,128)}) custom-call(bf16[121,128]{1,0:T(8,128)(2,1)S(1)} %get-tuple-element.6.refs_0_, f32[4,2048]{1,0:T(4,128)S(1)} %get-tuple-element.7.refs_1_, f32[9,128]{1,0:T(8,128)S(1)} %get-tuple-element.8.refs_2_), custom_call_target="tpu_custom_call" | custom-call | tf_op jit(solution)/shard_map/pallas_call | solution.py:381
